TPU v7x, 512 devices: a whole 4x8x8 slice. The times are simulated.
512 devices in a mesh: row: 64 (over z, x, y_hi), col: 8 (over y_lo, core).
Axes of the slice: x: 4, y: 8 (y_hi: 2, y_lo: 4; y = y_hi * 4 + y_lo), z: 8, core: 2. Of those that a mesh axis runs over, the one named last changes fastest.
Arguments:
- row_embed: bfloat16 [256, 256, 256], P('row', 'col')
- col_embed: bfloat16 [32, 256, 256], P('col', 'row')
- row_length: int32 [256], P('row'), may hold values from 32 to 256, as said below
- col_length: int32 [32], P('col'), may hold values from 32 to 256, as said below
- pair_valid: int32 [256, 32], P('row', 'col'), may hold values 0 or 1
- temper: float32 [8], replicated, may hold values from 0.05 to 0.25
- row_vector: float32 [256], replicated, may hold values from -0.375 to 0.375
- col_vector: float32 [256], replicated, may hold values from -0.375 to 0.375
Outputs:
- row_score: float32 [256, 256], P('row', 'col')
- col_score: float32 [32, 256], P('col', 'row')
Inputs may be any that keep to these rules, and one draw needn't show every extreme that they name: `row_length`: every length is at least 32; in every draw some row protein and some column protein have exactly 256 residues. `col_length`: every length is at least 32; some column protein has exactly 256 residues.
All inputs are finite; a program needn't handle non-finite values. No bound on the sum of `pair_valid` on one device may be relied on, other than what follows from the above.
Results may differ from a plain program's by a relative error of at most 0.0004.
Values may be sent and summed in bfloat16 or wider, within the bound.
A program may use at most 64 MiB of HBM per device.

v0:
```python
import math

import jax
import jax.numpy as jnp
from jax import lax
from jax.sharding import PartitionSpec as P

far_below = -1e30


def split_heads(block_rows, head_count):
    return block_rows.reshape(block_rows.shape[0], head_count, block_rows.shape[1] // head_count)


def pair_scores(query_rows, key_rows, temper):
    head_count = temper.shape[0]
    raw_scores = jnp.einsum(
        "ahd,bhd->hab",
        split_heads(query_rows, head_count),
        split_heads(key_rows, head_count),
        preferred_element_type=jnp.float32,
    )
    return raw_scores * temper[:, None, None]


def weights_along(scores, valid_mask, along_axis):
    masked = jnp.where(valid_mask, scores, far_below)
    peak_value = jnp.max(masked, axis=along_axis, keepdims=True)
    raised = jnp.where(valid_mask, jnp.exp(masked - peak_value), 0.0)
    return (raised / jnp.sum(raised, axis=along_axis, keepdims=True)).astype(jnp.bfloat16)


def readout(attended, own_rows, vector):
    return jnp.sum(jnp.tanh(attended + own_rows.astype(jnp.float32)) * vector, axis=-1)


def column_side(scores, query_rows, key_rows, row_len, col_len, temper, col_vector):
    head_count = temper.shape[0]
    row_pos = jnp.arange(query_rows.shape[0])
    col_pos = jnp.arange(key_rows.shape[0])
    toward_rows = weights_along(scores, (row_pos < row_len)[None, :, None], 1)
    col_out = jnp.einsum(
        "hab,ahd->bhd",
        toward_rows,
        split_heads(query_rows, head_count),
        preferred_element_type=jnp.float32,
    ).reshape(key_rows.shape)
    return jnp.where(col_pos < col_len, readout(col_out, key_rows, col_vector), 0.0)


def pair_terms(query_rows, key_rows, row_len, col_len, temper, row_vector, col_vector):
    head_count = temper.shape[0]
    scores = pair_scores(query_rows, key_rows, temper)
    row_pos = jnp.arange(query_rows.shape[0])
    col_pos = jnp.arange(key_rows.shape[0])
    toward_cols = weights_along(scores, (col_pos < col_len)[None, None, :], 2)
    row_out = jnp.einsum(
        "hab,bhd->ahd",
        toward_cols,
        split_heads(key_rows, head_count),
        preferred_element_type=jnp.float32,
    ).reshape(query_rows.shape)
    row_term = jnp.where(row_pos < row_len, readout(row_out, query_rows, row_vector), 0.0)
    col_term = column_side(scores, query_rows, key_rows, row_len, col_len, temper, col_vector)
    return (row_term, col_term)


def body(row_embed, col_embed, row_length, col_length, pair_valid, temper, row_vector, col_vector):
    row_block = lax.all_gather(row_embed, "col", axis=1, tiled=True)
    n_rows = row_block.shape[0]
    n_cols = col_embed.shape[0]
    length = row_block.shape[1]
    weight = pair_valid.astype(jnp.float32)
    pair_list = jnp.arange(n_rows * n_cols)
    col_block = lax.all_gather(col_embed, "row", axis=1, tiled=True)

    def one_pair(pair_index):
        row_pick = pair_index // n_cols
        col_pick = pair_index % n_cols
        return pair_terms(
            row_block[row_pick],
            col_block[col_pick],
            row_length[row_pick],
            col_length[col_pick],
            temper,
            row_vector,
            col_vector,
        )

    row_terms, col_terms = lax.map(one_pair, pair_list)
    row_terms = row_terms.reshape(n_rows, n_cols, length)
    col_terms = col_terms.reshape(n_rows, n_cols, length)
    row_total = jnp.sum(row_terms * weight[:, :, None], axis=1)
    col_total = jnp.sum(col_terms * weight[:, :, None], axis=0)
    row_scale = 1.0 / math.sqrt(n_cols * lax.axis_size("col"))
    col_scale = 1.0 / math.sqrt(n_rows * lax.axis_size("row"))
    row_score = lax.psum_scatter(row_total, "col", scatter_dimension=1, tiled=True) * row_scale
    col_score = lax.psum_scatter(col_total, "row", scatter_dimension=1, tiled=True) * col_scale
    return (row_score, col_score)


def solution(mesh):
    in_specs = (
        P("row", "col", None),
        P("col", "row", None),
        P("row"),
        P("col"),
        P("row", "col"),
        P(),
        P(),
        P(),
    )
    out_specs = (P("row", "col"), P("col", "row"))
    return jax.shard_map(body, mesh=mesh, in_specs=in_specs, out_specs=out_specs, check_vma=False)
```

profile of v0, /device:TPU:32, one launch (start us, length us, event | category | flops | bytes accessed | tf_op | source)
XLA Modules:
  0.0 651.0 jit_solution(17561862087583551523)
XLA Ops:
  8.2 14.9 %all_gather.7 = bf16[4,256,256]{2,0,1:T(4,128)(2,1)S(1)} all-gather(bf16[4,32,256]{2,0,1:T(4,128)(2,1)S(1)} %copy.13), channel_id=1, replica_groups=mesh['row'=64,'col'=8] {'col'}, dimensions={1}, use_global_device_ids=true | all-gather | bytes 589824 | tf_op jit(solution)/shard_map/all_gather | solution.py:69
  24.1 223.5 %all_gather.6 = bf16[4,256,256]{2,0,1:T(4,128)(2,1)S(1)} all-gather(bf16[4,4,256]{2,0,1:T(4,128)(2,1)S(1)} %copy.12), channel_id=1, replica_groups=mesh['row'=64,'col'=8] {'row'}, dimensions={1}, use_global_device_ids=true | all-gather | bytes 532480 | tf_op jit(solution)/shard_map/all_gather | solution.py:75
  247.9 165.9 %while.14 = (s32[]{:T(128)}, f32[16,256]{1,0:T(8,128)S(1)}, f32[16,256]{1,0:T(8,128)S(1)}, s32[16]{0:T(128)S(1)}, s32[4]{0:T(128)S(1)}, /*index=5*/bf16[4,256,25...) while((s32[]{:T(128)}, f32[16,256]{1,0:T(8,128)S(1)}, ...), condition=%wide.region_7.8_spmd, body=%wide.region_0.7_spmd.sunk | while | flops 142083616 | bytes 10012192 | solution.py:90
  252.6 1.0 fusion.50
  255.9 1.1 fusion.48
  266.3 1.1 fusion.48
  273.3 1.0 fusion.50
  276.7 1.0 fusion.48
  287.0 1.0 fusion.48
  294.1 1.0 fusion.50
  297.4 1.1 fusion.48
  307.8 1.1 fusion.48
  318.1 1.0 fusion.48
  328.5 1.0 fusion.48
  338.9 1.1 fusion.48
  349.2 1.1 fusion.48
  359.6 1.0 fusion.48
  370.0 1.0 fusion.48
  380.3 1.1 fusion.48
  390.7 1.1 fusion.48
  401.1 1.0 fusion.48
  411.5 1.0 fusion.48
  414.8 225.4 %all-reduce = f32[4,256]{1,0:T(4,128)S(1)} all-reduce(f32[4,256]{1,0:T(4,128)S(1)} %get-tuple-element.156), channel_id=3, replica_groups=mesh['row'=64,'col'=8] {'row'}, use_global_device_ids=true, to_apply=%region_11.12.clone | all-reduce | flops 1024 | bytes 8192
  640.2 1.3 dynamic-slice
  (267 shorter events, 108.4 us)
Async XLA Ops:
  7.2 240.7 %copy-start.3 = (s32[4]{0:T(128)S(1)}, s32[4]{0:T(128)}, u32[]{:S(2)}) copy-start(s32[4]{0:T(128)} %param.12) | copy-start | bytes 52
  7.2 240.7 %copy-start.4 = (s32[4]{0:T(128)S(1)}, s32[4]{0:T(128)}, u32[]{:S(2)}) copy-start(s32[4]{0:T(128)} %param.13) | copy-start | bytes 52
  7.2 240.7 %copy-start.5 = (f32[8]{0:T(128)S(1)}, f32[8]{0:T(128)}, u32[]{:S(2)}) copy-start(f32[8]{0:T(128)} %param.15) | copy-start | bytes 100
  7.2 240.7 %copy-start = (f32[256]{0:T(256)S(1)}, f32[256]{0:T(256)}, u32[]{:S(2)}) copy-start(f32[256]{0:T(256)} %param.16) | copy-start | bytes 3076
  7.2 240.7 %copy-start.1 = (f32[256]{0:T(256)S(1)}, f32[256]{0:T(256)}, u32[]{:S(2)}) copy-start(f32[256]{0:T(256)} %param.17) | copy-start | bytes 3076
  7.2 635.6 %reduce-scatter.5.cloned.1.call-start = ((), (), s32[]{:S(2)}) async-start(), calls=%async_computation.1 | async-start | bytes 147456
  247.9 166.0 %copy-start.2 = (s32[4,4]{1,0:T(4,128)S(1)}, s32[4,4]{1,0:T(4,128)}, u32[]{:S(2)}) copy-start(s32[4,4]{1,0:T(4,128)} %param.14) | copy-start | bytes 196
Sparse Core Ops, SparseCore 0:
  415.0 33.6 reduce-scatter.4
where the time goes:
time: 653 us; the launch traced here: 651 us
  blocking collectives  464 us (71%)
  matrix products  45.9 us (7%)
  other arithmetic  44.4 us (7%)
  loops' own time  43.1 us (7%)
  local copies, waits for them, and re-layouts  39.1 us (6%)
  between operations  14.8 us (2%)
    unnamed x1, blocking collectives  225 us
    all_gather x1, blocking collectives, body(): col_block = lax.all_gather(col_embed, 'row', axis=1, tiled=True)  223 us
    another operation x1, loops' own time, body(): row_terms, col_terms = lax.map(one_pair, pair_list)  43.1 us
    sub x32, matrix products, weights_along(): raised = jnp.where(valid_mask, jnp.exp(masked - peak_value), 0.0)  32.2 us
    all_gather x1, blocking collectives, body(): row_block = lax.all_gather(row_embed, 'col', axis=1, tiled=True)  14.9 us
  transfers between devices with their start and end apart: 1, of which 0 were waited for; matrix products, arithmetic and copies ran while one was open for 0% of the time, Pallas kernels for 0%

commit v1 on v0

v1 whole, which is shorter than its diff:
```python
import functools
import math

import jax
import jax.numpy as jnp
from jax import lax
from jax.experimental import pallas as pl
from jax.experimental.pallas import tpu as pltpu
from jax.sharding import PartitionSpec as P

MESH = pl.DeviceIdType.MESH
f32 = jnp.float32
bf16 = jnp.bfloat16
LOG2E = math.log2(math.e)

N_ROW = 64
N_COL = 8
R = 4
C = 4
L = 256
H = 256
NH = 8
D = H // NH
HT = 128 // D
STEPS = 2 * (C // 2) * R


def dot(a, b):
    return jnp.dot(a, b, preferred_element_type=f32)


def dot_t(a, b):
    return lax.dot_general(a, b, (((1,), (1,)), ((), ())), preferred_element_type=f32)


def kernel(
    row_hbm, col_in, row_len, col_len, valid, temper, row_vec, col_vec,
    row_out, col_out,
    col_own, row_buf, col_buf, col_nat,
    ql, kt, qt, vt, qf, kf, rv, cv,
    scores, e_row, e_col, row_acc, col_acc,
    row_res, row_got, col_msg, col_got,
    row_send, row_recv, col_send, col_recv, rres_send, rres_recv, cres_send, cres_recv,
):
    r = lax.axis_index("row")
    c = lax.axis_index("col")

    def row_peer(k):
        return (lax.rem(r + k, N_ROW), c)

    def col_peer(k):
        return (r, lax.rem(c + k, N_COL))

    barrier = pltpu.get_barrier_semaphore()

    def greet_row(k, _):
        pl.semaphore_signal(barrier, inc=1, device_id=row_peer(k), device_id_type=MESH)
        return 0

    def greet_col(k, _):
        pl.semaphore_signal(barrier, inc=1, device_id=col_peer(k), device_id_type=MESH)
        return 0

    lax.fori_loop(1, N_ROW, greet_row, 0)
    lax.fori_loop(1, N_COL, greet_col, 0)

    for j in range(C):
        kf[0, j, 0:4, 0:H] = col_in[j].astype(f32)
    for t in range(2):
        own = jnp.concatenate([kf[0, j, 0:4, t * 128:(t + 1) * 128] for j in range(C)], axis=0)
        col_own[t] = own.astype(bf16)

    rv[...] = jnp.broadcast_to(row_vec[...], (L, H)).T.reshape(NH, D, L)
    cv[...] = jnp.broadcast_to(col_vec[...], (L, H)).T.reshape(NH, D, L)
    row_acc[...] = jnp.zeros_like(row_acc)
    col_acc[...] = jnp.zeros_like(col_acc)

    pl.semaphore_wait(barrier, N_ROW - 1 + N_COL - 1)

    own_rows = pl.ds(pl.multiple_of(c * 32, 32), 32)
    for t in range(2):
        half = pl.ds(t * 128, 128)

        def send_col(k, _):
            pltpu.make_async_remote_copy(
                src_ref=col_own.at[t], dst_ref=col_buf.at[t, r],
                send_sem=col_send, recv_sem=col_recv.at[t],
                device_id=row_peer(k), device_id_type=MESH).start()
            return 0

        def send_row(k, _):
            pltpu.make_async_remote_copy(
                src_ref=row_hbm.at[:, :, half], dst_ref=row_buf.at[t, :, own_rows, :],
                send_sem=row_send, recv_sem=row_recv.at[t],
                device_id=col_peer(k), device_id_type=MESH).start()
            return 0

        lax.fori_loop(1, N_COL, send_row, 0)
        lax.fori_loop(1, N_ROW, send_col, 0)
        pltpu.make_async_copy(row_hbm.at[:, :, half], row_buf.at[t, :, own_rows, :], row_recv.at[t]).start()
        pltpu.make_async_copy(col_own.at[t], col_buf.at[t, r], col_recv.at[t]).start()

    lane = lax.broadcasted_iota(jnp.int32, (1, L), 1)
    sub = lax.broadcasted_iota(jnp.int32, (L, 1), 0)
    lane128 = lax.broadcasted_iota(jnp.int32, (1, 128), 1)

    def prepare_rows(t):
        pltpu.make_async_copy(row_buf.at[t], row_buf.at[t], row_recv.at[t]).wait()
        scale = jnp.zeros((1, 128), f32)
        for g in range(HT):
            scale = jnp.where(lane128 // D == g, temper[t * HT + g] * LOG2E, scale)

        def one(i, _):
            q = row_buf[t, i].astype(f32)
            ok = sub < row_len[i]
            filled = jnp.where(ok, q, q[0:1]) * scale
            hi = filled.astype(bf16).astype(f32)
            lo = filled - hi
            for g in range(HT):
                mine = lane128 // D == g
                ql[i, t * HT + g, :, 0:128] = jnp.where(mine, hi, 0.0).astype(bf16)
                ql[i, t * HT + g, :, 128:256] = jnp.where(mine, lo, 0.0).astype(bf16)
            flat = jnp.where(ok, q, 0.0).T
            ones = jnp.where(lane < row_len[i], 1.0, 0.0)
            pad = jnp.zeros((15, L), f32)
            for g in range(HT):
                own = flat[g * D:(g + 1) * D]
                qf[i, t * HT + g] = own
                qt[i, t * HT + g] = jnp.concatenate([own, ones, pad], axis=0).astype(bf16)
            return 0

        lax.fori_loop(0, R, one, 0)

    def prepare_cols(t):
        pltpu.make_async_copy(col_buf.at[t], col_buf.at[t], col_recv.at[t]).wait()
        o = lax.broadcasted_iota(jnp.int32, (256, 256), 0)
        m = lax.broadcasted_iota(jnp.int32, (256, 256), 1)
        source = lax.rem(o // 4, 16) * 16 + (o // 64) * 4 + lax.rem(o, 4)
        order = jnp.where(m == source, 1.0, 0.0).astype(bf16)
        for g in range(4):
            block = col_buf[t, g * 16:(g + 1) * 16].reshape(256, 128)
            moved = dot(order, block).astype(bf16)
            for j in range(C):
                col_nat[j, g * 64:(g + 1) * 64, :] = moved[j * 64:(j + 1) * 64]
        eye = jnp.where(lax.broadcasted_iota(jnp.int32, (128, 128), 0)
                        == lax.broadcasted_iota(jnp.int32, (128, 128), 1), 1.0, 0.0).astype(bf16)
        pad = jnp.zeros((15, L), f32)
        for j in range(C):
            flat = dot_t(eye, col_nat[j])
            ok = lane < col_len[j]
            filled = jnp.where(ok, flat, flat[:, 0:1]).astype(bf16)
            span = pl.ds((j % 2) * L, L)
            kt[j // 2, t, 0:128, span] = filled
            kt[j // 2, t, 128:256, span] = filled
            flat = jnp.where(ok, flat, 0.0)
            ones = jnp.where(ok, 1.0, 0.0)
            for g in range(HT):
                own = flat[g * D:(g + 1) * D]
                kf[j // 2, t * HT + g, :, span] = own
                vt[j, t * HT + g] = jnp.concatenate([own, ones, pad], axis=0).astype(bf16)

    def place(s):
        s = jnp.maximum(s, 0)
        return s // (2 * R), lax.rem(s // R, 2), lax.rem(s, R)

    def stage_scores(s, g):
        t, jp, i = place(s)
        scores[g] = dot(ql[i, t * HT + g], kt[jp, t])

    def stage_weights(g):
        for u in range(2):
            block = scores[g, :, u * L:(u + 1) * L]
            e_row[g, u] = jnp.exp2(block - jnp.max(block, axis=1, keepdims=True)).astype(bf16)
            e_col[g, :, u * L:(u + 1) * L] = jnp.exp2(block - jnp.max(block, axis=0, keepdims=True)).astype(bf16)

    def readout(product, own, vector):
        term = jnp.tanh(product[:D] * (1.0 / product[D:D + 1]) + own) * vector
        return term[0:8] + term[8:16] + term[16:24] + term[24:32]

    def stage_sums(s, g):
        t, jp, i = place(s)
        h = t * HT + g
        toward_rows = dot(qt[i, h], e_col[g])
        sides = [dot_t(vt[jp * 2 + u, h], e_row[g, u]) for u in range(2)]
        real = s >= 0
        for u in range(2):
            weight = valid[i, jp * 2 + u].astype(f32)
            span = pl.ds(u * L, L)
            row_term = readout(sides[u], qf[i, h], rv[h]) * weight
            col_term = readout(toward_rows[:, u * L:(u + 1) * L], kf[jp, h, :, span], cv[h]) * weight
            row_acc[i] += jnp.where(real, row_term, 0.0)
            col_acc[jp, :, span] += jnp.where(real, col_term, 0.0)

    prepare_rows(0)
    prepare_cols(0)

    def step(s, _):
        @pl.when(s == STEPS // 2)
        def _():
            prepare_rows(1)
            prepare_cols(1)

        for g in range(HT):
            stage_scores(s, g)
            stage_weights((g + 3) % 4)
            stage_sums(s if g >= 2 else s - 1, (g + 2) % 4)
        return 0

    lax.fori_loop(0, STEPS, step, 0)
    stage_weights(3)
    stage_sums(STEPS - 1, 2)
    stage_sums(STEPS - 1, 3)

    row_scale = 1.0 / math.sqrt(C * N_COL)
    col_scale = 1.0 / math.sqrt(R * N_ROW)
    for i in range(R):
        total = jnp.sum(row_acc[i], axis=0, keepdims=True) * row_scale
        total = jnp.where(lane < row_len[i], total, 0.0)
        for t in range(2):
            row_res[t, i:i + 1, :] = total[:, t * 128:(t + 1) * 128]
    row_res[:, R:8, :] = jnp.zeros((2, 8 - R, 128), f32)

    dest = lax.broadcasted_iota(jnp.int32, (N_ROW, L), 0)
    slot = lax.broadcasted_iota(jnp.int32, (N_ROW, L), 1)
    mine = slot // 4 == dest
    from_b = lax.broadcasted_iota(jnp.int32, (L, 128), 0)
    to_lane = lax.broadcasted_iota(jnp.int32, (L, 128), 1)
    msg = jnp.zeros((N_ROW, 128), f32)
    for j in range(C):
        total = jnp.sum(col_acc[j // 2, :, (j % 2) * L:(j % 2 + 1) * L], axis=0, keepdims=True) * col_scale
        total = jnp.where(lane < col_len[j], total, 0.0)
        spread = jnp.where(mine, total, 0.0)
        pick = jnp.where(to_lane == j * 4 + lax.rem(from_b, 4), 1.0, 0.0)
        msg = msg + jnp.dot(spread, pick, precision=lax.Precision.HIGHEST, preferred_element_type=f32)
    col_msg[...] = msg.reshape(N_ROW, 1, 128)

    def send_col_res(k, _):
        to = lax.rem(r + k, N_ROW)
        pltpu.make_async_remote_copy(
            src_ref=col_msg.at[to], dst_ref=col_got.at[r],
            send_sem=cres_send, recv_sem=cres_recv,
            device_id=(to, c), device_id_type=MESH).start()
        return 0

    def send_row_res(k, _):
        to = lax.rem(c + k, N_COL)
        pltpu.make_async_remote_copy(
            src_ref=row_res.at[to // 4], dst_ref=row_got.at[c],
            send_sem=rres_send, recv_sem=rres_recv,
            device_id=(r, to), device_id_type=MESH).start()
        return 0

    lax.fori_loop(1, N_ROW, send_col_res, 0)
    lax.fori_loop(1, N_COL, send_row_res, 0)
    pltpu.make_async_copy(col_msg.at[r], col_got.at[r], cres_recv).start()
    pltpu.make_async_copy(row_res.at[c // 4], row_got.at[c], rres_recv).start()

    pltpu.make_async_copy(row_got, row_got, rres_recv).wait()
    total = row_got[0]
    for k in range(1, N_COL):
        total = total + row_got[k]
    quarter = lax.rem(c, 4)
    answer = total[0:R, 0:32]
    for g in range(1, 4):
        answer = jnp.where(quarter == g, total[0:R, g * 32:(g + 1) * 32], answer)
    row_out[...] = answer

    pltpu.make_async_copy(col_got, col_got, cres_recv).wait()
    total = jnp.sum(col_got[...], axis=0)
    for j in range(C):
        col_out[j:j + 1, :] = total[:, j * 4:(j + 1) * 4]

    for t in range(2):
        others = pl.ds(0, N_ROW - 1)
        pltpu.make_async_copy(col_buf.at[t, others], col_buf.at[t, others], col_send).wait()
        most = pl.ds(0, 32 * (N_COL - 1))
        pltpu.make_async_copy(row_buf.at[t, :, most, :], row_buf.at[t, :, most, :], row_send).wait()
    others = pl.ds(0, N_ROW - 1)
    pltpu.make_async_copy(col_got.at[others], col_got.at[others], cres_send).wait()
    others = pl.ds(0, N_COL - 1)
    pltpu.make_async_copy(row_got.at[others], row_got.at[others], rres_send).wait()


def body(row_embed, col_embed, row_length, col_length, pair_valid, temper, row_vector, col_vector):
    vmem = pl.BlockSpec(memory_space=pltpu.VMEM)
    smem = pl.BlockSpec(memory_space=pltpu.SMEM)
    hbm = pl.BlockSpec(memory_space=pl.ANY)
    dma = pltpu.SemaphoreType.DMA
    return pl.pallas_call(
        kernel,
        out_shape=[jax.ShapeDtypeStruct((R, 32), f32), jax.ShapeDtypeStruct((C, 4), f32)],
        in_specs=[hbm, vmem, smem, smem, smem, smem, vmem, vmem],
        out_specs=[vmem, vmem],
        scratch_shapes=[
            pltpu.VMEM((2, 16, 128), bf16),
            pltpu.VMEM((2, R, L, 128), bf16),
            pltpu.VMEM((2, N_ROW, 16, 128), bf16),
            pltpu.VMEM((C, L, 128), bf16),
            pltpu.VMEM((R, NH, L, 256), bf16),
            pltpu.VMEM((C // 2, 2, 256, 2 * L), bf16),
            pltpu.VMEM((R, NH, 48, L), bf16),
            pltpu.VMEM((C, NH, 48, L), bf16),
            pltpu.VMEM((R, NH, D, L), f32),
            pltpu.VMEM((C // 2, NH, D, 2 * L), f32),
            pltpu.VMEM((NH, D, L), f32),
            pltpu.VMEM((NH, D, L), f32),
            pltpu.VMEM((HT, L, 2 * L), f32),
            pltpu.VMEM((HT, 2, L, L), bf16),
            pltpu.VMEM((HT, L, 2 * L), bf16),
            pltpu.VMEM((R, 8, L), f32),
            pltpu.VMEM((C // 2, 8, 2 * L), f32),
            pltpu.VMEM((2, 8, 128), f32),
            pltpu.VMEM((N_COL, 8, 128), f32),
            pltpu.VMEM((N_ROW, 1, 128), f32),
            pltpu.VMEM((N_ROW, 1, 128), f32),
            dma, dma((2,)), dma, dma((2,)), dma, dma, dma, dma,
        ],
        compiler_params=pltpu.CompilerParams(
            collective_id=0, has_side_effects=True, vmem_limit_bytes=48 * 2**20),
    )(row_embed, col_embed, row_length, col_length, pair_valid, temper,
      row_vector.reshape(1, H), col_vector.reshape(1, H))


def solution(mesh):
    in_specs = (
        P("row", "col", None),
        P("col", "row", None),
        P("row"),
        P("col"),
        P("row", "col"),
        P(),
        P(),
        P(),
    )
    out_specs = (P("row", "col"), P("col", "row"))
    return jax.shard_map(body, mesh=mesh, in_specs=in_specs, out_specs=out_specs, check_vma=False)
```

time: 653 us -> 74.9 us (0.11)
  the two profiles are of different devices: /device:TPU:32 before, /device:TPU:57 now
where the time goes in v1:
time: 74.9 us; the launch traced here: 74.6 us
  Pallas kernels  68.6 us (92%)
  local copies, waits for them, and re-layouts  5.36 us (7%)
    pallas_call x1, Pallas kernels, body(): pl.pallas_call(kernel, out_shape=[jax.ShapeDtypeStruct((R, 32), f32), jax...  68.6 us
    unnamed x18, local copies, waits for them, and re-layouts  5.36 us

profile of v1, /device:TPU:57, one launch (start us, length us, event | category | flops | bytes accessed | tf_op | source)
XLA Modules:
  0.0 74.6 jit_solution(13749321929945676253)
XLA Ops:
  0.6 0.0 copy-start.2
  0.6 0.0 copy-start.3
  0.7 0.0 copy-start.5
  0.7 0.7 copy-done.2
  1.3 0.0 copy-done.3
  1.3 0.0 copy-done.5
  1.3 0.0 copy-start
  1.3 0.8 %copy-done = bf16[4,32,256]{2,1,0:T(8,128)(2,1)S(1)} copy-done((bf16[4,32,256]{2,1,0:T(8,128)(2,1)S(1)}, bf16[4,32,256]{2,1,0:T(8,128)(2,1)}, u32[]{:S(2)}) %copy-start) | copy-done | bytes 65560
  2.2 0.0 copy-start.1
  2.2 0.7 copy-done.1
  2.9 0.0 copy-start.4
  2.9 0.7 copy-done.4
  3.5 0.0 copy-start.6
  3.6 0.7 copy-done.6
  4.2 0.0 copy-start.7
  4.2 0.7 copy-done.7
  4.9 68.6 %shard_map.95 = (f32[4,32]{1,0:T(4,128)S(1)}, f32[4,4]{1,0:T(4,128)S(1)}) custom-call(bf16[4,32,256]{2,1,0:T(8,128)(2,1)S(1)} %copy-done, bf16[4,4,256]{2,1,0:T(4,128)(2,1)S(1)} %copy-done.1, s32[4]{0:T(128)S(1)} %copy-done.5, s32[4]{0:T(128)S(1)} %copy-done.6, s32[4,4]{1,0:T(4,128)S(1)} %copy-done.2, f32[8]{0:T(128)S(1)} %copy-done.7, ...), custom_call_target="tpu_custom_call" | custom-call | tf_op jit(solution)/shard_map/pallas_call | solution.py:289
  73.5 0.6 copy.12
  74.1 0.6 copy.13
Async XLA Ops:
  0.6 0.7 copy-start.2
  0.6 0.7 copy-start.3
  0.7 0.7 copy-start.5
  1.3 0.8 %copy-start = (bf16[4,32,256]{2,1,0:T(8,128)(2,1)S(1)}, bf16[4,32,256]{2,1,0:T(8,128)(2,1)}, u32[]{:S(2)}) copy-start(bf16[4,32,256]{2,1,0:T(8,128)(2,1)} %row_hbm.1) | copy-start | bytes 196612
  2.2 0.7 copy-start.1
  2.9 0.7 copy-start.4
  3.5 0.7 copy-start.6
  4.2 0.7 copy-start.7

commit v2 on v1

--- a/solution.py
+++ b/solution.py
@@ -34,85 +34,159 @@
 
 
 def kernel(
-    row_hbm, col_in, row_len, col_len, valid, temper, row_vec, col_vec,
+    row_hbm, col_hbm, row_len_hbm, col_len_hbm, valid_hbm, temper_hbm, row_vec_hbm, col_vec_hbm,
     row_out, col_out,
-    col_own, row_buf, col_buf, col_nat,
+    col_in, row_len, col_len, valid, temper, row_vec, col_vec,
+    row_buf, col_buf, col_nat,
     ql, kt, qt, vt, qf, kf, rv, cv,
     scores, e_row, e_col, row_acc, col_acc,
     row_res, row_got, col_msg, col_got,
-    row_send, row_recv, col_send, col_recv, rres_send, rres_recv, cres_send, cres_recv,
+    in_sem, far_send, far_recv, near_send, near_recv, row_send, row_recv, twin_send, twin_recv, own_sem,
+    rres_send, rres_recv, cres_send, cres_recv,
 ):
     r = lax.axis_index("row")
     c = lax.axis_index("col")
-
-    def row_peer(k):
-        return (lax.rem(r + k, N_ROW), c)
-
-    def col_peer(k):
-        return (r, lax.rem(c + k, N_COL))
+    z, x, yh = r // 8, lax.rem(r // 2, 4), lax.rem(r, 2)
+    yl, core = c // 2, lax.rem(c, 2)
+    zh = z // 4
+
+    def device(dz, dx, dyh):
+        return (lax.rem(z + dz, 8) * 8 + lax.rem(x + dx, 4) * 2 + lax.rem(yh + dyh, 2), c)
+
+    def near(k, back):
+        two = jnp.where((core == 0) != back, 2, 6)
+        kz = k // 4
+        dz = jnp.where(kz == 3, two, jnp.where(kz == 2, 7, kz))
+        dx = lax.rem(k, 4)
+        return device(dz, 4 - dx if back else dx, 0)
+
+    def far(k):
+        return device((k // 2) * 4, 0, lax.rem(k, 2))
+
+    def along(k):
+        return (r, lax.rem(yl + k, 4) * 2 + core)
+
+    twin = (r, yl * 2 + 1 - core)
+
+    small = [(col_hbm, col_in), (row_len_hbm, row_len), (col_len_hbm, col_len), (valid_hbm, valid),
+             (temper_hbm, temper), (row_vec_hbm, row_vec), (col_vec_hbm, col_vec)]
+    copies = [pltpu.make_async_copy(src, dst, in_sem.at[n]) for n, (src, dst) in enumerate(small)]
+    for copy in copies:
+        copy.start()
+    own_rows = pl.ds(pl.multiple_of(core * 128 + yl * 32, 32), 32)
+    own_row_copy = pltpu.make_async_copy(row_hbm, row_buf.at[:, own_rows, :], own_sem)
+    own_row_copy.start()
 
     barrier = pltpu.get_barrier_semaphore()
 
-    def greet_row(k, _):
-        pl.semaphore_signal(barrier, inc=1, device_id=row_peer(k), device_id_type=MESH)
+    def greet(target):
+        pl.semaphore_signal(barrier, inc=1, device_id=target, device_id_type=MESH)
         return 0
 
-    def greet_col(k, _):
-        pl.semaphore_signal(barrier, inc=1, device_id=col_peer(k), device_id_type=MESH)
+    lax.fori_loop(1, 4, lambda k, _: greet(far(k)), 0)
+    lax.fori_loop(1, 16, lambda k, _: greet(near(k, True)), 0)
+    lax.fori_loop(1, 4, lambda k, _: greet(along(k)), 0)
+    greet(twin)
+
+    for copy in copies:
+        copy.wait()
+    block = (lax.rem(z, 4) * 4 + x) * 4
+    slot = block + zh * 2 + yh
+    own = jnp.concatenate([col_in[j].astype(f32) for j in range(C)], axis=0).astype(bf16)
+    for t in range(2):
+        col_buf[t, slot] = own[:, t * 128:(t + 1) * 128]
+
+    pl.semaphore_wait(barrier, 22)
+
+    def send_far(k, _):
+        pltpu.make_async_remote_copy(
+            src_ref=col_buf.at[:, slot], dst_ref=col_buf.at[:, slot],
+            send_sem=far_send, recv_sem=far_recv.at[k - 1],
+            device_id=far(k), device_id_type=MESH).start()
         return 0
 
-    lax.fori_loop(1, N_ROW, greet_row, 0)
-    lax.fori_loop(1, N_COL, greet_col, 0)
-
-    for j in range(C):
-        kf[0, j, 0:4, 0:H] = col_in[j].astype(f32)
-    for t in range(2):
-        own = jnp.concatenate([kf[0, j, 0:4, t * 128:(t + 1) * 128] for j in range(C)], axis=0)
-        col_own[t] = own.astype(bf16)
+    lax.fori_loop(1, 4, send_far, 0)
+
+    def send_rows(t):
+        half = pl.ds(t * 128, 128)
+
+        def one(k, _):
+            pltpu.make_async_remote_copy(
+                src_ref=row_hbm.at[:, :, half], dst_ref=row_buf.at[:, own_rows, half],
+                send_sem=row_send, recv_sem=row_recv.at[t],
+                device_id=along(k), device_id_type=MESH).start()
+            return 0
+
+        lax.fori_loop(1, 4, one, 0)
+
+    def send_near(t, part):
+        pair = pl.ds(block + part * 2, 2)
+
+        def one(k, _):
+            pltpu.make_async_remote_copy(
+                src_ref=col_buf.at[t, pair], dst_ref=col_buf.at[t, pair],
+                send_sem=near_send, recv_sem=near_recv.at[t],
+                device_id=near(k, False), device_id_type=MESH).start()
+            return 0
+
+        lax.fori_loop(1, 16, one, 0)
+
+    same_core = pl.ds(pl.multiple_of(core * 128, 128), 128)
+
+    def pass_rows(t):
+        half = pl.ds(t * 128, 128)
+        three = row_buf.at[:, pl.ds(0, 96), half]
+        pltpu.make_async_copy(three, three, row_recv.at[t]).wait()
+        pltpu.make_async_remote_copy(
+            src_ref=row_buf.at[:, same_core, half], dst_ref=row_buf.at[:, same_core, half],
+            send_sem=twin_send, recv_sem=twin_recv.at[t],
+            device_id=twin, device_id_type=MESH).start()
+
+    def await_far(k):
+        pltpu.make_async_copy(col_buf.at[:, 0], col_buf.at[:, 0], far_recv.at[k - 1]).wait()
+
+    send_rows(0)
+    send_rows(1)
+    await_far(1)
+    send_near(0, zh)
+    await_far(2)
+    await_far(3)
+    send_near(0, 1 - zh)
+    own_row_copy.wait()
+    pass_rows(0)
+    send_near(1, zh)
+    send_near(1, 1 - zh)
+    pass_rows(1)
 
     rv[...] = jnp.broadcast_to(row_vec[...], (L, H)).T.reshape(NH, D, L)
     cv[...] = jnp.broadcast_to(col_vec[...], (L, H)).T.reshape(NH, D, L)
     row_acc[...] = jnp.zeros_like(row_acc)
     col_acc[...] = jnp.zeros_like(col_acc)
 
-    pl.semaphore_wait(barrier, N_ROW - 1 + N_COL - 1)
-
-    own_rows = pl.ds(pl.multiple_of(c * 32, 32), 32)
-    for t in range(2):
+    def row_residue(place):
+        return (lax.rem(place // 32, 4) * 2 + place // 128) * 32 + lax.rem(place, 32)
+
+    def col_residue(place):
+        s = place // 4
+        device_z = s // 16 + lax.rem(s // 2, 2) * 4
+        return ((device_z * 4 + lax.rem(s // 4, 4)) * 2 + lax.rem(s, 2)) * 4 + lax.rem(place, 4)
+
+    lane = lax.broadcasted_iota(jnp.int32, (1, L), 1)
+    row_lane, col_lane = row_residue(lane), col_residue(lane)
+    row_sub = row_residue(lax.broadcasted_iota(jnp.int32, (L, 1), 0))
+    lane128 = lax.broadcasted_iota(jnp.int32, (1, 128), 1)
+
+    def prepare_rows(t):
         half = pl.ds(t * 128, 128)
-
-        def send_col(k, _):
-            pltpu.make_async_remote_copy(
-                src_ref=col_own.at[t], dst_ref=col_buf.at[t, r],
-                send_sem=col_send, recv_sem=col_recv.at[t],
-                device_id=row_peer(k), device_id_type=MESH).start()
-            return 0
-
-        def send_row(k, _):
-            pltpu.make_async_remote_copy(
-                src_ref=row_hbm.at[:, :, half], dst_ref=row_buf.at[t, :, own_rows, :],
-                send_sem=row_send, recv_sem=row_recv.at[t],
-                device_id=col_peer(k), device_id_type=MESH).start()
-            return 0
-
-        lax.fori_loop(1, N_COL, send_row, 0)
-        lax.fori_loop(1, N_ROW, send_col, 0)
-        pltpu.make_async_copy(row_hbm.at[:, :, half], row_buf.at[t, :, own_rows, :], row_recv.at[t]).start()
-        pltpu.make_async_copy(col_own.at[t], col_buf.at[t, r], col_recv.at[t]).start()
-
-    lane = lax.broadcasted_iota(jnp.int32, (1, L), 1)
-    sub = lax.broadcasted_iota(jnp.int32, (L, 1), 0)
-    lane128 = lax.broadcasted_iota(jnp.int32, (1, 128), 1)
-
-    def prepare_rows(t):
-        pltpu.make_async_copy(row_buf.at[t], row_buf.at[t], row_recv.at[t]).wait()
+        theirs = row_buf.at[:, pl.ds(0, 128), half]
+        pltpu.make_async_copy(theirs, theirs, twin_recv.at[t]).wait()
         scale = jnp.zeros((1, 128), f32)
         for g in range(HT):
             scale = jnp.where(lane128 // D == g, temper[t * HT + g] * LOG2E, scale)
 
         def one(i, _):
-            q = row_buf[t, i].astype(f32)
-            ok = sub < row_len[i]
+            q = row_buf[i, :, half].astype(f32)
+            ok = row_sub < row_len[i]
             filled = jnp.where(ok, q, q[0:1]) * scale
             hi = filled.astype(bf16).astype(f32)
             lo = filled - hi
@@ -121,7 +195,7 @@
                 ql[i, t * HT + g, :, 0:128] = jnp.where(mine, hi, 0.0).astype(bf16)
                 ql[i, t * HT + g, :, 128:256] = jnp.where(mine, lo, 0.0).astype(bf16)
             flat = jnp.where(ok, q, 0.0).T
-            ones = jnp.where(lane < row_len[i], 1.0, 0.0)
+            ones = jnp.where(row_lane < row_len[i], 1.0, 0.0)
             pad = jnp.zeros((15, L), f32)
             for g in range(HT):
                 own = flat[g * D:(g + 1) * D]
@@ -132,7 +206,8 @@
         lax.fori_loop(0, R, one, 0)
 
     def prepare_cols(t):
-        pltpu.make_async_copy(col_buf.at[t], col_buf.at[t], col_recv.at[t]).wait()
+        theirs = col_buf.at[t, pl.ds(0, 60)]
+        pltpu.make_async_copy(theirs, theirs, near_recv.at[t]).wait()
         o = lax.broadcasted_iota(jnp.int32, (256, 256), 0)
         m = lax.broadcasted_iota(jnp.int32, (256, 256), 1)
         source = lax.rem(o // 4, 16) * 16 + (o // 64) * 4 + lax.rem(o, 4)
@@ -147,7 +222,7 @@
         pad = jnp.zeros((15, L), f32)
         for j in range(C):
             flat = dot_t(eye, col_nat[j])
-            ok = lane < col_len[j]
+            ok = col_lane < col_len[j]
             filled = jnp.where(ok, flat, flat[:, 0:1]).astype(bf16)
             span = pl.ds((j % 2) * L, L)
             kt[j // 2, t, 0:128, span] = filled
@@ -215,51 +290,55 @@
     col_scale = 1.0 / math.sqrt(R * N_ROW)
     for i in range(R):
         total = jnp.sum(row_acc[i], axis=0, keepdims=True) * row_scale
-        total = jnp.where(lane < row_len[i], total, 0.0)
+        total = jnp.where(row_lane < row_len[i], total, 0.0)
         for t in range(2):
             row_res[t, i:i + 1, :] = total[:, t * 128:(t + 1) * 128]
     row_res[:, R:8, :] = jnp.zeros((2, 8 - R, 128), f32)
 
     dest = lax.broadcasted_iota(jnp.int32, (N_ROW, L), 0)
-    slot = lax.broadcasted_iota(jnp.int32, (N_ROW, L), 1)
-    mine = slot // 4 == dest
+    mine = lax.broadcasted_iota(jnp.int32, (N_ROW, L), 1) // 4 == dest
     from_b = lax.broadcasted_iota(jnp.int32, (L, 128), 0)
     to_lane = lax.broadcasted_iota(jnp.int32, (L, 128), 1)
     msg = jnp.zeros((N_ROW, 128), f32)
     for j in range(C):
         total = jnp.sum(col_acc[j // 2, :, (j % 2) * L:(j % 2 + 1) * L], axis=0, keepdims=True) * col_scale
-        total = jnp.where(lane < col_len[j], total, 0.0)
+        total = jnp.where(col_lane < col_len[j], total, 0.0)
         spread = jnp.where(mine, total, 0.0)
         pick = jnp.where(to_lane == j * 4 + lax.rem(from_b, 4), 1.0, 0.0)
         msg = msg + jnp.dot(spread, pick, precision=lax.Precision.HIGHEST, preferred_element_type=f32)
     col_msg[...] = msg.reshape(N_ROW, 1, 128)
 
     def send_col_res(k, _):
-        to = lax.rem(r + k, N_ROW)
+        n, m = k // 8, lax.rem(k, 8)
+        dz = lax.rem(12 + jnp.where(lax.rem(n, 2) == 1, -((n + 1) // 2), n // 2), 8)
+        dx, dyh = lax.rem(m // 2 + 2, 4), lax.rem(m + 1, 2)
+        to_z, to_x, to_yh = lax.rem(z + dz, 8), lax.rem(x + dx, 4), lax.rem(yh + dyh, 2)
+        place = (lax.rem(to_z, 4) * 4 + to_x) * 4 + (to_z // 4) * 2 + to_yh
         pltpu.make_async_remote_copy(
-            src_ref=col_msg.at[to], dst_ref=col_got.at[r],
+            src_ref=col_msg.at[place], dst_ref=col_got.at[r],
             send_sem=cres_send, recv_sem=cres_recv,
-            device_id=(to, c), device_id_type=MESH).start()
+            device_id=device(dz, dx, dyh), device_id_type=MESH).start()
         return 0
 
     def send_row_res(k, _):
         to = lax.rem(c + k, N_COL)
         pltpu.make_async_remote_copy(
-            src_ref=row_res.at[to // 4], dst_ref=row_got.at[c],
+            src_ref=row_res.at[lax.rem(to, 2)], dst_ref=row_got.at[c],
             send_sem=rres_send, recv_sem=rres_recv,
             device_id=(r, to), device_id_type=MESH).start()
         return 0
 
-    lax.fori_loop(1, N_ROW, send_col_res, 0)
+    lax.fori_loop(0, 61, send_col_res, 0)
+    lax.fori_loop(62, 64, send_col_res, 0)
     lax.fori_loop(1, N_COL, send_row_res, 0)
-    pltpu.make_async_copy(col_msg.at[r], col_got.at[r], cres_recv).start()
-    pltpu.make_async_copy(row_res.at[c // 4], row_got.at[c], rres_recv).start()
+    pltpu.make_async_copy(col_msg.at[slot], col_got.at[r], cres_recv).start()
+    pltpu.make_async_copy(row_res.at[core], row_got.at[c], rres_recv).start()
 
     pltpu.make_async_copy(row_got, row_got, rres_recv).wait()
     total = row_got[0]
     for k in range(1, N_COL):
         total = total + row_got[k]
-    quarter = lax.rem(c, 4)
+    quarter = yl
     answer = total[0:R, 0:32]
     for g in range(1, 4):
         answer = jnp.where(quarter == g, total[0:R, g * 32:(g + 1) * 32], answer)
@@ -270,11 +349,15 @@
     for j in range(C):
         col_out[j:j + 1, :] = total[:, j * 4:(j + 1) * 4]
 
+    three = col_buf.at[:, pl.ds(0, 3)]
+    pltpu.make_async_copy(three, three, far_send).wait()
     for t in range(2):
-        others = pl.ds(0, N_ROW - 1)
-        pltpu.make_async_copy(col_buf.at[t, others], col_buf.at[t, others], col_send).wait()
-        most = pl.ds(0, 32 * (N_COL - 1))
-        pltpu.make_async_copy(row_buf.at[t, :, most, :], row_buf.at[t, :, most, :], row_send).wait()
+        sixty = col_buf.at[t, pl.ds(0, 60)]
+        pltpu.make_async_copy(sixty, sixty, near_send).wait()
+    most = row_buf.at[:, pl.ds(0, 96), :]
+    pltpu.make_async_copy(most, most, row_send).wait()
+    most = row_buf.at[:, pl.ds(0, 128), :]
+    pltpu.make_async_copy(most, most, twin_send).wait()
     others = pl.ds(0, N_ROW - 1)
     pltpu.make_async_copy(col_got.at[others], col_got.at[others], cres_send).wait()
     others = pl.ds(0, N_COL - 1)
@@ -283,17 +366,22 @@
 
 def body(row_embed, col_embed, row_length, col_length, pair_valid, temper, row_vector, col_vector):
     vmem = pl.BlockSpec(memory_space=pltpu.VMEM)
-    smem = pl.BlockSpec(memory_space=pltpu.SMEM)
-    hbm = pl.BlockSpec(memory_space=pl.ANY)
+    hbm = pl.BlockSpec(memory_space=pltpu.HBM)
     dma = pltpu.SemaphoreType.DMA
     return pl.pallas_call(
         kernel,
         out_shape=[jax.ShapeDtypeStruct((R, 32), f32), jax.ShapeDtypeStruct((C, 4), f32)],
-        in_specs=[hbm, vmem, smem, smem, smem, smem, vmem, vmem],
+        in_specs=[hbm] * 8,
         out_specs=[vmem, vmem],
         scratch_shapes=[
-            pltpu.VMEM((2, 16, 128), bf16),
-            pltpu.VMEM((2, R, L, 128), bf16),
+            pltpu.VMEM((C, 4, H), bf16),
+            pltpu.SMEM((R,), jnp.int32),
+            pltpu.SMEM((C,), jnp.int32),
+            pltpu.SMEM((R, C), jnp.int32),
+            pltpu.SMEM((NH,), f32),
+            pltpu.VMEM((1, H), f32),
+            pltpu.VMEM((1, H), f32),
+            pltpu.VMEM((R, L, H), bf16),
             pltpu.VMEM((2, N_ROW, 16, 128), bf16),
             pltpu.VMEM((C, L, 128), bf16),
             pltpu.VMEM((R, NH, L, 256), bf16),
@@ -313,10 +401,11 @@
             pltpu.VMEM((N_COL, 8, 128), f32),
             pltpu.VMEM((N_ROW, 1, 128), f32),
             pltpu.VMEM((N_ROW, 1, 128), f32),
-            dma, dma((2,)), dma, dma((2,)), dma, dma, dma, dma,
+            dma((7,)), dma, dma((3,)), dma, dma((2,)), dma, dma((2,)), dma, dma((2,)), dma,
+            dma, dma, dma, dma,
         ],
         compiler_params=pltpu.CompilerParams(
-            collective_id=0, has_side_effects=True, vmem_limit_bytes=48 * 2**20),
+            collective_id=0, has_side_effects=True, vmem_limit_bytes=64 * 2**20),
     )(row_embed, col_embed, row_length, col_length, pair_valid, temper,
       row_vector.reshape(1, H), col_vector.reshape(1, H))
 

time: 74.9 us -> 63.1 us (0.84)
  the two profiles are of different devices: /device:TPU:57 before, /device:TPU:8 now
where the time goes in v2:
time: 63.1 us; the launch traced here: 62.9 us
  Pallas kernels  60.4 us (96%)
  local copies, waits for them, and re-layouts  1.89 us (3%)
  between operations  0.65 us (1%)
    pallas_call x1, Pallas kernels, body(): pl.pallas_call(kernel, out_shape=[jax.ShapeDtypeStruct((R, 32), f32), jax...  60.4 us
    unnamed x6, local copies, waits for them, and re-layouts  1.89 us

profile of v2, /device:TPU:8, one launch (start us, length us, event | category | flops | bytes accessed | tf_op | source)
XLA Modules:
  0.0 62.9 jit_solution(9639850006979734864)
XLA Ops:
  0.6 60.4 %shard_map.95 = (f32[4,32]{1,0:T(4,128)}, f32[4,4]{1,0:T(4,128)}) custom-call(bf16[4,32,256]{2,1,0:T(8,128)(2,1)} %row_hbm.1, bf16[4,4,256]{2,1,0:T(4,128)(2,1)} %col_hbm.1, s32[4]{0:T(128)} %row_len_hbm.1, s32[4]{0:T(128)} %col_len_hbm.1, s32[4,4]{1,0:T(4,128)} %valid_hbm.1, f32[8]{0:T(128)} %temper_hbm.1, f32[1,256]{1,0:T(1,128)} %bitcast.2, f32[1,256]{1,0:T(1,128)} %bitcast.3), custom_call_target="tpu_custom_call" | custom-call | tf_op jit(solution)/shard_map/pallas_call | solution.py:371
  61.0 0.0 copy-start.1
  61.0 0.7 %copy-done.1 = f32[4,32]{1,0:T(4,128)S(1)} copy-done((f32[4,32]{1,0:T(4,128)S(1)}, f32[4,32]{1,0:T(4,128)}, u32[]{:S(2)}) %copy-start.1) | copy-done | bytes 536
  61.7 0.0 copy-start
  61.7 0.6 copy.12
  62.3 0.1 copy-done
  62.4 0.6 copy.13
Async XLA Ops:
  61.0 0.7 %copy-start.1 = (f32[4,32]{1,0:T(4,128)S(1)}, f32[4,32]{1,0:T(4,128)}, u32[]{:S(2)}) copy-start(f32[4,32]{1,0:T(4,128)} %get-tuple-element.4) | copy-start | bytes 1540
  61.7 0.7 %copy-start = (f32[4,4]{1,0:T(4,128)S(1)}, f32[4,4]{1,0:T(4,128)}, u32[]{:S(2)}) copy-start(f32[4,4]{1,0:T(4,128)} %get-tuple-element.5) | copy-start | bytes 196

commit v3 on v2

--- a/solution.py
+++ b/solution.py
@@ -23,6 +23,7 @@
 D = H // NH
 HT = 128 // D
 STEPS = 2 * (C // 2) * R
+UNROLL = 4
 
 
 def dot(a, b):
@@ -35,7 +36,7 @@
 
 def kernel(
     row_hbm, col_hbm, row_len_hbm, col_len_hbm, valid_hbm, temper_hbm, row_vec_hbm, col_vec_hbm,
-    row_out, col_out,
+    out,
     col_in, row_len, col_len, valid, temper, row_vec, col_vec,
     row_buf, col_buf, col_nat,
     ql, kt, qt, vt, qf, kf, rv, cv,
@@ -54,14 +55,12 @@
         return (lax.rem(z + dz, 8) * 8 + lax.rem(x + dx, 4) * 2 + lax.rem(yh + dyh, 2), c)
 
     def near(k, back):
-        two = jnp.where((core == 0) != back, 2, 6)
         kz = k // 4
-        dz = jnp.where(kz == 3, two, jnp.where(kz == 2, 7, kz))
+        dz = jnp.where(kz == 3, jnp.where((core == 0) != back, 2, 6), jnp.where(kz == 2, 7, kz))
         dx = lax.rem(k, 4)
         return device(dz, 4 - dx if back else dx, 0)
 
-    def far(k):
-        return device((k // 2) * 4, 0, lax.rem(k, 2))
+    other_y, other_z = device(0, 0, 1), device(4, 0, 0)
 
     def along(k):
         return (r, lax.rem(yl + k, 4) * 2 + core)
@@ -83,7 +82,8 @@
         pl.semaphore_signal(barrier, inc=1, device_id=target, device_id_type=MESH)
         return 0
 
-    lax.fori_loop(1, 4, lambda k, _: greet(far(k)), 0)
+    greet(other_y)
+    greet(other_z)
     lax.fori_loop(1, 16, lambda k, _: greet(near(k, True)), 0)
     lax.fori_loop(1, 4, lambda k, _: greet(along(k)), 0)
     greet(twin)
@@ -92,20 +92,17 @@
         copy.wait()
     block = (lax.rem(z, 4) * 4 + x) * 4
     slot = block + zh * 2 + yh
-    own = jnp.concatenate([col_in[j].astype(f32) for j in range(C)], axis=0).astype(bf16)
-    for t in range(2):
-        col_buf[t, slot] = own[:, t * 128:(t + 1) * 128]
-
-    pl.semaphore_wait(barrier, 22)
-
-    def send_far(k, _):
+    col_buf[slot] = jnp.concatenate([col_in[j].astype(f32) for j in range(C)], axis=0).astype(bf16)
+
+    pl.semaphore_wait(barrier, 21)
+
+    def send_far(span, n, target):
         pltpu.make_async_remote_copy(
-            src_ref=col_buf.at[:, slot], dst_ref=col_buf.at[:, slot],
-            send_sem=far_send, recv_sem=far_recv.at[k - 1],
-            device_id=far(k), device_id_type=MESH).start()
-        return 0
-
-    lax.fori_loop(1, 4, send_far, 0)
+            src_ref=col_buf.at[span], dst_ref=col_buf.at[span],
+            send_sem=far_send.at[n], recv_sem=far_recv.at[n],
+            device_id=target, device_id_type=MESH).start()
+
+    send_far(pl.ds(slot, 1), 0, other_y)
 
     def send_rows(t):
         half = pl.ds(t * 128, 128)
@@ -119,17 +116,21 @@
 
         lax.fori_loop(1, 4, one, 0)
 
-    def send_near(t, part):
+    def send_near(part):
         pair = pl.ds(block + part * 2, 2)
 
         def one(k, _):
             pltpu.make_async_remote_copy(
-                src_ref=col_buf.at[t, pair], dst_ref=col_buf.at[t, pair],
-                send_sem=near_send, recv_sem=near_recv.at[t],
+                src_ref=col_buf.at[pair], dst_ref=col_buf.at[pair],
+                send_sem=near_send, recv_sem=near_recv,
                 device_id=near(k, False), device_id_type=MESH).start()
             return 0
 
         lax.fori_loop(1, 16, one, 0)
+
+    def await_far(n):
+        theirs = col_buf.at[pl.ds(0, n + 1)]
+        pltpu.make_async_copy(theirs, theirs, far_recv.at[n]).wait()
 
     same_core = pl.ds(pl.multiple_of(core * 128, 128), 128)
 
@@ -142,20 +143,15 @@
             send_sem=twin_send, recv_sem=twin_recv.at[t],
             device_id=twin, device_id_type=MESH).start()
 
-    def await_far(k):
-        pltpu.make_async_copy(col_buf.at[:, 0], col_buf.at[:, 0], far_recv.at[k - 1]).wait()
-
     send_rows(0)
     send_rows(1)
-    await_far(1)
-    send_near(0, zh)
-    await_far(2)
-    await_far(3)
-    send_near(0, 1 - zh)
+    await_far(0)
+    send_far(pl.ds(block + zh * 2, 2), 1, other_z)
+    send_near(zh)
     own_row_copy.wait()
     pass_rows(0)
-    send_near(1, zh)
-    send_near(1, 1 - zh)
+    await_far(1)
+    send_near(1 - zh)
     pass_rows(1)
 
     rv[...] = jnp.broadcast_to(row_vec[...], (L, H)).T.reshape(NH, D, L)
@@ -206,15 +202,13 @@
         lax.fori_loop(0, R, one, 0)
 
     def prepare_cols(t):
-        theirs = col_buf.at[t, pl.ds(0, 60)]
-        pltpu.make_async_copy(theirs, theirs, near_recv.at[t]).wait()
         o = lax.broadcasted_iota(jnp.int32, (256, 256), 0)
         m = lax.broadcasted_iota(jnp.int32, (256, 256), 1)
         source = lax.rem(o // 4, 16) * 16 + (o // 64) * 4 + lax.rem(o, 4)
         order = jnp.where(m == source, 1.0, 0.0).astype(bf16)
         for g in range(4):
-            block = col_buf[t, g * 16:(g + 1) * 16].reshape(256, 128)
-            moved = dot(order, block).astype(bf16)
+            piece = col_buf[g * 16:(g + 1) * 16, :, t * 128:(t + 1) * 128].reshape(256, 128)
+            moved = dot(order, piece).astype(bf16)
             for j in range(C):
                 col_nat[j, g * 64:(g + 1) * 64, :] = moved[j * 64:(j + 1) * 64]
         eye = jnp.where(lax.broadcasted_iota(jnp.int32, (128, 128), 0)
@@ -267,21 +261,25 @@
             col_acc[jp, :, span] += jnp.where(real, col_term, 0.0)
 
     prepare_rows(0)
+    prepare_rows(1)
+    theirs = col_buf.at[pl.ds(0, 60)]
+    pltpu.make_async_copy(theirs, theirs, near_recv).wait()
     prepare_cols(0)
 
-    def step(s, _):
-        @pl.when(s == STEPS // 2)
+    def steps(n, _):
+        @pl.when(n == STEPS // UNROLL // 2)
         def _():
-            prepare_rows(1)
             prepare_cols(1)
 
-        for g in range(HT):
-            stage_scores(s, g)
-            stage_weights((g + 3) % 4)
-            stage_sums(s if g >= 2 else s - 1, (g + 2) % 4)
+        for i in range(UNROLL):
+            s = n * UNROLL + i
+            for g in range(HT):
+                stage_scores(s, g)
+                stage_weights((g + 3) % 4)
+                stage_sums(s if g >= 2 else s - 1, (g + 2) % 4)
         return 0
 
-    lax.fori_loop(0, STEPS, step, 0)
+    lax.fori_loop(0, STEPS // UNROLL, steps, 0)
     stage_weights(3)
     stage_sums(STEPS - 1, 2)
     stage_sums(STEPS - 1, 3)
@@ -297,15 +295,22 @@
 
     dest = lax.broadcasted_iota(jnp.int32, (N_ROW, L), 0)
     mine = lax.broadcasted_iota(jnp.int32, (N_ROW, L), 1) // 4 == dest
-    from_b = lax.broadcasted_iota(jnp.int32, (L, 128), 0)
-    to_lane = lax.broadcasted_iota(jnp.int32, (L, 128), 1)
-    msg = jnp.zeros((N_ROW, 128), f32)
+    from_b = lax.broadcasted_iota(jnp.int32, (3 * L, 128), 0)
+    to_lane = lax.broadcasted_iota(jnp.int32, (3 * L, 128), 1)
+    pick = jnp.where(to_lane == lax.rem(from_b, 4), 1.0, 0.0).astype(bf16)
+    spread = []
     for j in range(C):
         total = jnp.sum(col_acc[j // 2, :, (j % 2) * L:(j % 2 + 1) * L], axis=0, keepdims=True) * col_scale
         total = jnp.where(col_lane < col_len[j], total, 0.0)
-        spread = jnp.where(mine, total, 0.0)
-        pick = jnp.where(to_lane == j * 4 + lax.rem(from_b, 4), 1.0, 0.0)
-        msg = msg + jnp.dot(spread, pick, precision=lax.Precision.HIGHEST, preferred_element_type=f32)
+        parts = []
+        for _ in range(3):
+            parts.append(total.astype(bf16).astype(f32))
+            total = total - parts[-1]
+        spread.append(jnp.concatenate([jnp.where(mine, part, 0.0).astype(bf16) for part in parts], axis=1))
+    picked = dot(jnp.concatenate(spread, axis=0), pick)
+    msg = picked[0:N_ROW]
+    for j in range(1, C):
+        msg = msg + pltpu.roll(picked[j * N_ROW:(j + 1) * N_ROW], 4 * j, 1)
     col_msg[...] = msg.reshape(N_ROW, 1, 128)
 
     def send_col_res(k, _):
@@ -342,18 +347,18 @@
     answer = total[0:R, 0:32]
     for g in range(1, 4):
         answer = jnp.where(quarter == g, total[0:R, g * 32:(g + 1) * 32], answer)
-    row_out[...] = answer
+    out[0:R, 0:32] = answer
 
     pltpu.make_async_copy(col_got, col_got, cres_recv).wait()
     total = jnp.sum(col_got[...], axis=0)
     for j in range(C):
-        col_out[j:j + 1, :] = total[:, j * 4:(j + 1) * 4]
-
-    three = col_buf.at[:, pl.ds(0, 3)]
-    pltpu.make_async_copy(three, three, far_send).wait()
-    for t in range(2):
-        sixty = col_buf.at[t, pl.ds(0, 60)]
-        pltpu.make_async_copy(sixty, sixty, near_send).wait()
+        out[R + j:R + j + 1, 0:4] = total[:, j * 4:(j + 1) * 4]
+
+    for n in range(2):
+        sent = col_buf.at[pl.ds(0, n + 1)]
+        pltpu.make_async_copy(sent, sent, far_send.at[n]).wait()
+    sent = col_buf.at[pl.ds(0, 60)]
+    pltpu.make_async_copy(sent, sent, near_send).wait()
     most = row_buf.at[:, pl.ds(0, 96), :]
     pltpu.make_async_copy(most, most, row_send).wait()
     most = row_buf.at[:, pl.ds(0, 128), :]
@@ -368,11 +373,11 @@
     vmem = pl.BlockSpec(memory_space=pltpu.VMEM)
     hbm = pl.BlockSpec(memory_space=pltpu.HBM)
     dma = pltpu.SemaphoreType.DMA
-    return pl.pallas_call(
+    result = pl.pallas_call(
         kernel,
-        out_shape=[jax.ShapeDtypeStruct((R, 32), f32), jax.ShapeDtypeStruct((C, 4), f32)],
+        out_shape=jax.ShapeDtypeStruct((R + C, 128), f32),
         in_specs=[hbm] * 8,
-        out_specs=[vmem, vmem],
+        out_specs=vmem,
         scratch_shapes=[
             pltpu.VMEM((C, 4, H), bf16),
             pltpu.SMEM((R,), jnp.int32),
@@ -382,7 +387,7 @@
             pltpu.VMEM((1, H), f32),
             pltpu.VMEM((1, H), f32),
             pltpu.VMEM((R, L, H), bf16),
-            pltpu.VMEM((2, N_ROW, 16, 128), bf16),
+            pltpu.VMEM((N_ROW, 16, H), bf16),
             pltpu.VMEM((C, L, 128), bf16),
             pltpu.VMEM((R, NH, L, 256), bf16),
             pltpu.VMEM((C // 2, 2, 256, 2 * L), bf16),
@@ -401,13 +406,14 @@
             pltpu.VMEM((N_COL, 8, 128), f32),
             pltpu.VMEM((N_ROW, 1, 128), f32),
             pltpu.VMEM((N_ROW, 1, 128), f32),
-            dma((7,)), dma, dma((3,)), dma, dma((2,)), dma, dma((2,)), dma, dma((2,)), dma,
+            dma((7,)), dma((2,)), dma((2,)), dma, dma, dma, dma((2,)), dma, dma((2,)), dma,
             dma, dma, dma, dma,
         ],
         compiler_params=pltpu.CompilerParams(
             collective_id=0, has_side_effects=True, vmem_limit_bytes=64 * 2**20),
     )(row_embed, col_embed, row_length, col_length, pair_valid, temper,
       row_vector.reshape(1, H), col_vector.reshape(1, H))
+    return result[:R, :32], result[R:, :4]
 
 
 def solution(mesh):

time: 63.1 us -> 61.3 us (0.971)
  Pallas kernels: 60.4 us -> 58.6 us
    slice x0 -> x2, local copies, waits for them, and re-layouts: none -> 1.89 us  [body(): return (result[:R, :32], result[R:, :4])]
    unnamed x6 -> x2, local copies, waits for them, and re-layouts: 1.89 us -> 0.01 us
    pallas_call x1, Pallas kernels: 60.4 us -> 58.6 us  [body(): pl.pallas_call(kernel, out_shape=jax.ShapeDtypeStruct((R + C, 128), f32),...]
where the time goes in v3:
time: 61.3 us; the launch traced here: 61.1 us
  Pallas kernels  58.6 us (96%)
  local copies, waits for them, and re-layouts  1.9 us (3%)
  between operations  0.65 us (1%)
    pallas_call x1, Pallas kernels, body(): pl.pallas_call(kernel, out_shape=jax.ShapeDtypeStruct((R + C, 128), f32),...  58.6 us
    slice x2, local copies, waits for them, and re-layouts, body(): return (result[:R, :32], result[R:, :4])  1.89 us

profile of v3, /device:TPU:8, one launch (start us, length us, event | category | flops | bytes accessed | tf_op | source)
XLA Modules:
  0.0 61.1 jit_solution(12315334669595783226)
XLA Ops:
  0.6 58.6 %shard_map.95 = f32[8,128]{1,0:T(8,128)} custom-call(bf16[4,32,256]{2,1,0:T(8,128)(2,1)} %row_hbm.1, bf16[4,4,256]{2,1,0:T(4,128)(2,1)} %col_hbm.1, s32[4]{0:T(128)} %row_len_hbm.1, s32[4]{0:T(128)} %col_len_hbm.1, s32[4,4]{1,0:T(4,128)} %valid_hbm.1, f32[8]{0:T(128)} %temper_hbm.1, f32[1,256]{1,0:T(1,128)} %bitcast.2, f32[1,256]{1,0:T(1,128)} %bitcast.3), custom_call_target="tpu_custom_call" | custom-call | tf_op jit(solution)/shard_map/pallas_call | solution.py:376
  59.2 0.0 copy-start
  59.2 1.3 %slice.7 = f32[4,4]{1,0:T(4,128)} slice(f32[8,128]{1,0:T(8,128)} %shard_map.95), slice={[4:8], [0:4]} | slice | bytes 128 | tf_op jit(solution)/shard_map/slice | solution.py:416
  60.5 0.0 copy-done
  60.5 0.6 slice.6
Async XLA Ops:
  59.2 1.3 %copy-start = (f32[8,128]{1,0:T(8,128)S(1)}, f32[8,128]{1,0:T(8,128)}, u32[]{:S(2)}) copy-start(f32[8,128]{1,0:T(8,128)} %shard_map.95) | copy-start | bytes 12292

commit v4 on v3

--- a/solution.py
+++ b/solution.py
@@ -41,7 +41,7 @@
     row_buf, col_buf, col_nat,
     ql, kt, qt, vt, qf, kf, rv, cv,
     scores, e_row, e_col, row_acc, col_acc,
-    row_res, row_got, col_msg, col_got,
+    row_res, row_got, col_msg, col_got, order, eye, pick,
     in_sem, far_send, far_recv, near_send, near_recv, row_send, row_recv, twin_send, twin_recv, own_sem,
     rres_send, rres_recv, cres_send, cres_recv,
 ):
@@ -67,6 +67,18 @@
 
     twin = (r, yl * 2 + 1 - core)
 
+    barrier = pltpu.get_barrier_semaphore()
+
+    def greet(target):
+        pl.semaphore_signal(barrier, inc=1, device_id=target, device_id_type=MESH)
+        return 0
+
+    greet(other_y)
+    greet(other_z)
+    lax.fori_loop(1, 16, lambda k, _: greet(near(k, True)), 0)
+    lax.fori_loop(1, 4, lambda k, _: greet(along(k)), 0)
+    greet(twin)
+
     small = [(col_hbm, col_in), (row_len_hbm, row_len), (col_len_hbm, col_len), (valid_hbm, valid),
              (temper_hbm, temper), (row_vec_hbm, row_vec), (col_vec_hbm, col_vec)]
     copies = [pltpu.make_async_copy(src, dst, in_sem.at[n]) for n, (src, dst) in enumerate(small)]
@@ -75,18 +87,6 @@
     own_rows = pl.ds(pl.multiple_of(core * 128 + yl * 32, 32), 32)
     own_row_copy = pltpu.make_async_copy(row_hbm, row_buf.at[:, own_rows, :], own_sem)
     own_row_copy.start()
-
-    barrier = pltpu.get_barrier_semaphore()
-
-    def greet(target):
-        pl.semaphore_signal(barrier, inc=1, device_id=target, device_id_type=MESH)
-        return 0
-
-    greet(other_y)
-    greet(other_z)
-    lax.fori_loop(1, 16, lambda k, _: greet(near(k, True)), 0)
-    lax.fori_loop(1, 4, lambda k, _: greet(along(k)), 0)
-    greet(twin)
 
     for copy in copies:
         copy.wait()
@@ -202,20 +202,14 @@
         lax.fori_loop(0, R, one, 0)
 
     def prepare_cols(t):
-        o = lax.broadcasted_iota(jnp.int32, (256, 256), 0)
-        m = lax.broadcasted_iota(jnp.int32, (256, 256), 1)
-        source = lax.rem(o // 4, 16) * 16 + (o // 64) * 4 + lax.rem(o, 4)
-        order = jnp.where(m == source, 1.0, 0.0).astype(bf16)
         for g in range(4):
             piece = col_buf[g * 16:(g + 1) * 16, :, t * 128:(t + 1) * 128].reshape(256, 128)
-            moved = dot(order, piece).astype(bf16)
+            moved = dot(order[...], piece).astype(bf16)
             for j in range(C):
                 col_nat[j, g * 64:(g + 1) * 64, :] = moved[j * 64:(j + 1) * 64]
-        eye = jnp.where(lax.broadcasted_iota(jnp.int32, (128, 128), 0)
-                        == lax.broadcasted_iota(jnp.int32, (128, 128), 1), 1.0, 0.0).astype(bf16)
         pad = jnp.zeros((15, L), f32)
         for j in range(C):
-            flat = dot_t(eye, col_nat[j])
+            flat = dot_t(eye[...], col_nat[j])
             ok = col_lane < col_len[j]
             filled = jnp.where(ok, flat, flat[:, 0:1]).astype(bf16)
             span = pl.ds((j % 2) * L, L)
@@ -262,6 +256,15 @@
 
     prepare_rows(0)
     prepare_rows(1)
+    o = lax.broadcasted_iota(jnp.int32, (256, 256), 0)
+    m = lax.broadcasted_iota(jnp.int32, (256, 256), 1)
+    source = lax.rem(o // 4, 16) * 16 + (o // 64) * 4 + lax.rem(o, 4)
+    order[...] = jnp.where(m == source, 1.0, 0.0).astype(bf16)
+    eye[...] = jnp.where(lax.broadcasted_iota(jnp.int32, (128, 128), 0)
+                         == lax.broadcasted_iota(jnp.int32, (128, 128), 1), 1.0, 0.0).astype(bf16)
+    from_b = lax.broadcasted_iota(jnp.int32, (3 * L, 128), 0)
+    to_lane = lax.broadcasted_iota(jnp.int32, (3 * L, 128), 1)
+    pick[...] = jnp.where(to_lane == lax.rem(from_b, 4), 1.0, 0.0).astype(bf16)
     theirs = col_buf.at[pl.ds(0, 60)]
     pltpu.make_async_copy(theirs, theirs, near_recv).wait()
     prepare_cols(0)
@@ -295,9 +298,6 @@
 
     dest = lax.broadcasted_iota(jnp.int32, (N_ROW, L), 0)
     mine = lax.broadcasted_iota(jnp.int32, (N_ROW, L), 1) // 4 == dest
-    from_b = lax.broadcasted_iota(jnp.int32, (3 * L, 128), 0)
-    to_lane = lax.broadcasted_iota(jnp.int32, (3 * L, 128), 1)
-    pick = jnp.where(to_lane == lax.rem(from_b, 4), 1.0, 0.0).astype(bf16)
     spread = []
     for j in range(C):
         total = jnp.sum(col_acc[j // 2, :, (j % 2) * L:(j % 2 + 1) * L], axis=0, keepdims=True) * col_scale
@@ -307,7 +307,7 @@
             parts.append(total.astype(bf16).astype(f32))
             total = total - parts[-1]
         spread.append(jnp.concatenate([jnp.where(mine, part, 0.0).astype(bf16) for part in parts], axis=1))
-    picked = dot(jnp.concatenate(spread, axis=0), pick)
+    picked = dot(jnp.concatenate(spread, axis=0), pick[...])
     msg = picked[0:N_ROW]
     for j in range(1, C):
         msg = msg + pltpu.roll(picked[j * N_ROW:(j + 1) * N_ROW], 4 * j, 1)
@@ -367,6 +367,11 @@
     pltpu.make_async_copy(col_got.at[others], col_got.at[others], cres_send).wait()
     others = pl.ds(0, N_COL - 1)
     pltpu.make_async_copy(row_got.at[others], row_got.at[others], rres_send).wait()
+
+
+def part_results(result, row_out, col_out):
+    row_out[...] = result[0:R, 0:32]
+    col_out[...] = result[R:R + C, 0:4]
 
 
 def body(row_embed, col_embed, row_length, col_length, pair_valid, temper, row_vector, col_vector):
@@ -406,6 +411,9 @@
             pltpu.VMEM((N_COL, 8, 128), f32),
             pltpu.VMEM((N_ROW, 1, 128), f32),
             pltpu.VMEM((N_ROW, 1, 128), f32),
+            pltpu.VMEM((256, 256), bf16),
+            pltpu.VMEM((128, 128), bf16),
+            pltpu.VMEM((3 * L, 128), bf16),
             dma((7,)), dma((2,)), dma((2,)), dma, dma, dma, dma((2,)), dma, dma((2,)), dma,
             dma, dma, dma, dma,
         ],
@@ -413,7 +421,12 @@
             collective_id=0, has_side_effects=True, vmem_limit_bytes=64 * 2**20),
     )(row_embed, col_embed, row_length, col_length, pair_valid, temper,
       row_vector.reshape(1, H), col_vector.reshape(1, H))
-    return result[:R, :32], result[R:, :4]
+    return pl.pallas_call(
+        part_results,
+        out_shape=[jax.ShapeDtypeStruct((R, 32), f32), jax.ShapeDtypeStruct((C, 4), f32)],
+        in_specs=[vmem],
+        out_specs=[vmem, vmem],
+    )(result)
 
 
 def solution(mesh):

time: 61.3 us -> 60.7 us (level)
  local copies, waits for them, and re-layouts: 1.9 us -> 0 us
  Pallas kernels: 58.6 us -> 59.8 us
    slice x2 -> x0, local copies, waits for them, and re-layouts: 1.89 us -> none  [body(): return (result[:R, :32], result[R:, :4])]
    pallas_call x0 -> x1, Pallas kernels: none -> 1.27 us  [body(): pl.pallas_call(part_results, out_shape=[jax.ShapeDtypeStruct((R, 32), f32...]
where the time goes in v4:
time: 60.7 us; the launch traced here: 60.5 us
  Pallas kernels  59.8 us (99%)
  between operations  0.64 us (1%)
    pallas_call x1, Pallas kernels, body(): pl.pallas_call(kernel, out_shape=jax.ShapeDtypeStruct((R + C, 128), f32),...  58.6 us
    pallas_call x1, Pallas kernels, body(): pl.pallas_call(part_results, out_shape=[jax.ShapeDtypeStruct((R, 32), f32...  1.27 us

profile of v4, /device:TPU:8, one launch (start us, length us, event | category | flops | bytes accessed | tf_op | source)
XLA Modules:
  0.0 60.5 jit_solution(11359206070868672785)
XLA Ops:
  0.6 58.6 %shard_map.95.result = f32[8,128]{1,0:T(8,128)} custom-call(bf16[4,32,256]{2,1,0:T(8,128)(2,1)} %row_hbm.1, bf16[4,4,256]{2,1,0:T(4,128)(2,1)} %col_hbm.1, s32[4]{0:T(128)} %row_len_hbm.1, s32[4]{0:T(128)} %col_len_hbm.1, s32[4,4]{1,0:T(4,128)} %valid_hbm.1, f32[8]{0:T(128)} %temper_hbm.1, f32[1,256]{1,0:T(1,128)} %bitcast.2, f32[1,256]{1,0:T(1,128)} %bitcast.3), custom_call_target="tpu_custom_call" | custom-call | tf_op jit(solution)/shard_map/pallas_call | solution.py:381
  59.2 1.3 %shard_map.96 = (f32[4,32]{1,0:T(4,128)}, f32[4,4]{1,0:T(4,128)}) custom-call(f32[8,128]{1,0:T(8,128)} %shard_map.95.result), custom_call_target="tpu_custom_call" | custom-call | tf_op jit(solution)/shard_map/pallas_call | solution.py:424

commit v5 on v4

--- a/solution.py
+++ b/solution.py
@@ -148,10 +148,10 @@
     await_far(0)
     send_far(pl.ds(block + zh * 2, 2), 1, other_z)
     send_near(zh)
+    await_far(1)
+    send_near(1 - zh)
     own_row_copy.wait()
     pass_rows(0)
-    await_far(1)
-    send_near(1 - zh)
     pass_rows(1)
 
     rv[...] = jnp.broadcast_to(row_vec[...], (L, H)).T.reshape(NH, D, L)

time: 60.7 us -> 60.7 us (level)
  no operation moved by 1% of the time
where the time goes in v5:
time: 60.7 us; the launch traced here: 60.5 us
  Pallas kernels  59.8 us (99%)
  between operations  0.64 us (1%)
    pallas_call x1, Pallas kernels, body(): pl.pallas_call(kernel, out_shape=jax.ShapeDtypeStruct((R + C, 128), f32),...  58.6 us
    pallas_call x1, Pallas kernels, body(): pl.pallas_call(part_results, out_shape=[jax.ShapeDtypeStruct((R, 32), f32...  1.27 us

profile of v5, /device:TPU:8, one launch (start us, length us, event | category | flops | bytes accessed | tf_op | source)
XLA Modules:
  0.0 60.5 jit_solution(1674203540089175736)
XLA Ops:
  0.6 58.6 %shard_map.95.result = f32[8,128]{1,0:T(8,128)} custom-call(bf16[4,32,256]{2,1,0:T(8,128)(2,1)} %row_hbm.1, bf16[4,4,256]{2,1,0:T(4,128)(2,1)} %col_hbm.1, s32[4]{0:T(128)} %row_len_hbm.1, s32[4]{0:T(128)} %col_len_hbm.1, s32[4,4]{1,0:T(4,128)} %valid_hbm.1, f32[8]{0:T(128)} %temper_hbm.1, f32[1,256]{1,0:T(1,128)} %bitcast.2, f32[1,256]{1,0:T(1,128)} %bitcast.3), custom_call_target="tpu_custom_call" | custom-call | tf_op jit(solution)/shard_map/pallas_call | solution.py:381
  59.2 1.3 %shard_map.96 = (f32[4,32]{1,0:T(4,128)}, f32[4,4]{1,0:T(4,128)}) custom-call(f32[8,128]{1,0:T(8,128)} %shard_map.95.result), custom_call_target="tpu_custom_call" | custom-call | tf_op jit(solution)/shard_map/pallas_call | solution.py:424
